TPU v7x, 32 devices: a whole 2x2x4 slice. The times are simulated.
32 devices in a mesh: dp: 8 (over y, x, core), layer: 4 (over z).
Axes of the slice: x: 2, y: 2, z: 4, core: 2. Of those that a mesh axis runs over, the one named last changes fastest.
Arguments:
- coords: float32 [3, 4096], P(None, ('dp', 'layer')), may hold values from -4 to 4
- sample_ids: int32 [4096], P(('dp', 'layer')), may hold values from 0 to 262143
- pool: float32 [2097152], P('dp'), may hold values from -6 to 6
- in_weight: float32 [3, 1024], replicated, may hold values from -3.5 to 3.5
- in_bias: float32 [1024], replicated, may hold values from -1 to 1
- hidden: bfloat16 [2, 1024, 1024], replicated, may hold values from -0.1875 to 0.1875
- out_weight: float32 [1024, 4], replicated, may hold values from -0.1875 to 0.1875
Outputs:
- update: bfloat16 [2, 1024, 1024], replicated
- point_loss: float32 [4096], P(('dp', 'layer'))
Inputs may be any that keep to these rules, and one draw needn't show every extreme that they name: sample_ids[p] is an offset into the pool block of 262144 entries held by dp index p // (128 * 4).
All inputs are finite; a program needn't handle non-finite values.
Results may differ from a plain program's by a relative error of at most 0.011.
Values may be sent and summed in bfloat16 or wider, within the bound.
A program may use at most 128 MiB of HBM per device.

v0:
```python
import jax
import jax.numpy as jnp
from jax import lax
from jax.sharding import PartitionSpec as P

VISCOSITY = 0.1
DAMPING = 0.1


def taylor_tanh(pre, pre_grad, pre_lap):
    act = jnp.tanh(pre)
    slope = 1.0 - act * act
    act_lap = slope * pre_lap - 2.0 * act * slope * jnp.sum(pre_grad * pre_grad, axis=0)
    return (act, slope * pre_grad, act_lap)


def network(nudges, coords, in_weight, in_bias, hidden, out_weight):
    count = coords.shape[1]
    width = in_weight.shape[1]
    pre = jnp.dot(coords.T, in_weight, precision=lax.Precision.HIGHEST) + in_bias
    pre_grad = jnp.broadcast_to(in_weight[:, None, :], (3, count, width))
    pre_lap = jnp.zeros((count, width), in_weight.dtype)
    stacks = []
    for level in range(hidden.shape[0]):
        act, act_grad, act_lap = taylor_tanh(pre, pre_grad, pre_lap)
        stack = (
            jnp.concatenate([act[None], act_grad, act_lap[None]], 0)
            .astype(jnp.bfloat16)
            .reshape(5 * count, width)
        )
        stacks.append(stack)
        mixed = jnp.dot(stack, hidden[level], preferred_element_type=jnp.float32) + nudges[level]
        mixed = mixed.reshape(5, count, width)
        pre, pre_grad, pre_lap = (mixed[0], mixed[1:4], mixed[4])
    act, act_grad, act_lap = taylor_tanh(pre, pre_grad, pre_lap)
    field = jnp.dot(act, out_weight, precision=lax.Precision.HIGHEST)
    field_grad = jnp.einsum("kpw,wc->kpc", act_grad, out_weight, precision=lax.Precision.HIGHEST)
    field_lap = jnp.dot(act_lap, out_weight, precision=lax.Precision.HIGHEST)
    return (field, field_grad, field_lap, stacks)


def residual_loss(field, field_grad, field_lap):
    velocity = field[:, :3].T
    advect = jnp.sum(velocity[:, :, None] * field_grad[:, :, :3], axis=0)
    momentum = advect + field_grad[:, :, 3].T - VISCOSITY * field_lap[:, :3]
    continuity = field_grad[0, :, 0] + field_grad[1, :, 1] + field_grad[2, :, 2]
    return 0.5 * (jnp.sum(momentum * momentum, axis=1) + continuity * continuity)


def point_terms(coords, weight, in_weight, in_bias, hidden, out_weight, total):
    count = coords.shape[1]
    width = in_weight.shape[1]
    zeros = [jnp.zeros((5 * count, width), jnp.float32) for level in range(hidden.shape[0])]

    def loss_of(nudges):
        field, field_grad, field_lap, stacks = network(
            nudges, coords, in_weight, in_bias, hidden, out_weight
        )
        losses = residual_loss(field, field_grad, field_lap)
        return (jnp.sum(weight * losses) / total, (losses, stacks))

    value, pull, extra = jax.vjp(loss_of, zeros, has_aux=True)
    losses, stacks = extra
    deltas = [piece.astype(jnp.bfloat16) for piece in pull(jnp.ones_like(value))[0]]
    return (losses, stacks, deltas)


def damped_inverse(factor, scale):
    size = factor.shape[-1]
    eye = jnp.eye(size, dtype=jnp.float32)
    damped = factor + DAMPING * scale * eye
    lower = jnp.linalg.cholesky(damped)
    return jax.scipy.linalg.cho_solve((lower, True), jnp.broadcast_to(eye, damped.shape))


def shards(coords, sample_ids, pool, in_weight, in_bias, hidden, out_weight):
    n_dp = lax.axis_size("dp")
    n_layer = lax.axis_size("layer")
    points_here = coords.shape[1]
    total = points_here * n_dp * n_layer
    width = hidden.shape[1]
    levels = hidden.shape[0]
    block = width // n_dp
    half_width = width // 2
    dp_index = lax.axis_index("dp")
    layer_index = lax.axis_index("layer")
    level_own = layer_index // 2
    kind_own = layer_index % 2
    weight = jax.nn.softplus(pool[sample_ids])
    losses, stacks, deltas = point_terms(
        coords, weight, in_weight, in_bias, hidden, out_weight, total
    )
    factor_list = []
    grad_list = []
    for level in range(levels):
        rows_a = stacks[level].reshape(-1, n_dp, block)
        rows_g = deltas[level].reshape(-1, n_dp, block)
        part_a = (
            jnp.einsum("rnb,rnc->nbc", rows_a, rows_a, preferred_element_type=jnp.float32) / total
        )
        part_g = (
            jnp.einsum("rnb,rnc->nbc", rows_g, rows_g, preferred_element_type=jnp.float32) * total
        )
        factor_list.append(jnp.stack([part_a, part_g], axis=1))
        halves = deltas[level].reshape(-1, 2, half_width)
        grad_list.append(
            jnp.einsum("rnb,rhc->nhbc", rows_a, halves, preferred_element_type=jnp.float32)
        )
    factor_terms = jnp.stack(factor_list, axis=1).reshape(n_dp * levels * 2, block * block)
    grad_terms = jnp.stack(grad_list, axis=1).reshape(n_dp * levels * 2 * block, half_width)
    owned = lax.psum_scatter(
        factor_terms, ("dp", "layer"), scatter_dimension=0, tiled=True
    ).reshape(block, block)
    own_trace = jnp.trace(owned)
    marked = jnp.where(jnp.arange(n_layer) == layer_index, own_trace, 0.0)
    totals = lax.psum(marked, ("dp", "layer"))
    inverse = damped_inverse(owned, totals[layer_index] / width)
    inverses = lax.all_gather(
        inverse.reshape(1, block * block), ("dp", "layer"), axis=0, tiled=True
    )
    inverses = inverses.reshape(n_dp, levels, 2, block, block)
    inv_a = inverses[dp_index, level_own, 0]
    inv_g_all = inverses[:, level_own, 1]
    inv_g = lax.dynamic_slice_in_dim(inv_g_all, kind_own * (n_dp // 2), n_dp // 2, 0)
    owned_grad = lax.psum_scatter(grad_terms, ("dp", "layer"), scatter_dimension=0, tiled=True)
    left = jnp.dot(inv_a, owned_grad, precision=lax.Precision.HIGHEST).reshape(
        block, n_dp // 2, block
    )
    right = jnp.einsum("ajc,jcq->ajq", left, inv_g, precision=lax.Precision.HIGHEST)
    update_block = right.reshape(1, block, half_width).astype(jnp.bfloat16)
    gathered = lax.all_gather(update_block, ("dp", "layer"), axis=0, tiled=True)
    update = (
        gathered.reshape(n_dp, levels, 2, block, half_width)
        .transpose(1, 0, 3, 2, 4)
        .reshape(levels, width, width)
    )
    return (update, losses)


def solution(mesh):
    return jax.shard_map(
        shards,
        mesh=mesh,
        in_specs=(P(None, ("dp", "layer")), P(("dp", "layer")), P("dp"), P(), P(), P(), P()),
        out_specs=(P(), P(("dp", "layer"))),
        check_vma=False,
    )
```

profile of v0, /device:TPU:9, one launch (start us, length us, event | category | flops | bytes accessed | tf_op | source)
XLA Modules:
  0.0 527.7 jit_solution(13886342239951749449)
XLA Ops:
  7.2 0.8 multiply_reduce_fusion.4
  8.0 1.4 multiply_subtract_fusion.2
  9.4 1.0 broadcast_multiply_fusion.1
  10.8 0.9 copy-done.20
  11.6 1.5 fusion.4
  13.6 1.0 copy-done.6
  14.7 0.8 copy-done.11
  16.1 1.5 fusion.2
  17.9 1.2 copy-done.15
  19.6 1.0 multiply_reduce_fusion.2
  20.7 1.4 fusion.15
  22.2 1.7 gather_fusion
  23.9 2.0 negate_multiply_fusion.2
  27.1 1.2 multiply_bitcast_fusion.1
  28.4 1.8 add_add_fusion.1
  30.2 2.1 fusion.40
  32.8 2.2 copy-done.21
  35.0 1.6 fusion.12
  37.8 1.7 multiply_bitcast_fusion
  40.5 0.7 fusion.28
  41.6 1.5 fusion.34
  43.1 1.4 copy.72
  44.6 2.1 copy.47
  48.0 1.4 copy.70
  49.5 3.0 copy.42
  52.5 2.4 fusion.43
  55.5 2.5 copy.101
  58.1 4.4 convert_element_type.107
  62.5 4.4 convert_element_type.108
  66.9 3.6 convolution_bitcast_fusion.1
  70.6 1.8 convolution_bitcast_fusion
  72.4 1.6 pad_maximum_fusion
  74.0 4.2 copy.58
  78.3 112.8 %all-reduce.16.cloned.1.call-done = f32[32,16384]{1,0:T(8,128)} async-done(((f32[32,16384]{1,0:T(8,128)}), f32[32,16384]{1,0:T(8,128)}) %all-reduce.16.cloned.1.call-update) | async-done | bytes 2097168
  191.1 1.8 fusion.67
  193.5 44.2 %psum.7 = f32[4]{0:T(128)S(1)} all-reduce(f32[4]{0:T(128)S(1)} %compare_select_fusion.3), channel_id=1, replica_groups=mesh['dp'=8,'layer'=4] {'dp','layer'}, use_global_device_ids=true, to_apply=%region_9.10 | all-reduce | flops 4 | bytes 32 | tf_op jit(solution)/shard_map/psum | solution.py:116
  239.2 11.7 %cholesky.18 = f32[128,128]{1,0:T(8,128)S(1)} custom-call(f32[128,128]{1,0:T(8,128)S(1)} %fusion.64), custom_call_target="Cholesky" | custom-call | tf_op jit(solution)/shard_map/jit(cholesky)/cholesky | solution.py:72
  252.2 9.8 %custom-call.10 = f32[1,128,128]{1,2,0:T(8,128)S(1)} custom-call(f32[1,128,128]{2,1,0:T(8,128)S(1)} %fusion.57), custom_call_target="InvertDiagBlocksLowerTriangular" | custom-call | tf_op jit(solution)/shard_map/jit(_cho_solve)/triangular_solve | solution.py:73
  262.3 0.8 fusion.60
  263.5 114.5 %reduce-scatter.2.cloned.1.call-done = f32[128,512]{1,0:T(8,128)} async-done(((f32[4096,512]{1,0:T(8,128)}), f32[128,512]{1,0:T(8,128)}) %reduce-scatter.2.cloned.1.call-update) | async-done | bytes 262160 | tf_op jit(solution)/shard_map/reduce_scatter | solution.py:125
  378.0 1.1 copy.68
  379.1 59.9 %all-gather.6.cloned.1.call-done = f32[32,1,16384]{2,1,0:T(1,128)} async-done(((f32[1,1,16384]{2,1,0:T(1,128)}), f32[32,1,16384]{2,1,0:T(1,128)}) %all-gather.6.cloned.1.call-update) | async-done | bytes 2097168 | tf_op jit(solution)/shard_map/all_gather | solution.py:118
  439.0 1.2 fusion.58
  440.2 1.6 convolution_convert_fusion
  441.8 0.8 copy.60
  442.6 62.1 %all-gather.4.cloned.1.call-done = bf16[32,128,512]{2,1,0:T(8,128)(2,1)} async-done(((bf16[1,128,512]{2,1,0:T(8,128)(2,1)}), bf16[32,128,512]{2,1,0:T(8,128)(2,1)}) %all-gather.4.cloned.1.call-update) | async-done | bytes 4194320 | tf_op jit(solution)/shard_map/all_gather | solution.py:131
  504.7 8.5 %copy.61 = bf16[2,8,128,2,512]{4,3,2,1,0:T(2,128)(2,1)} copy(bf16[2,8,128,2,512]{4,2,3,0,1:T(8,128)(2,1)} %bitcast.192) | data formatting | bytes 8388608 | tf_op jit(solution)/shard_map/transpose | solution.py:134
  513.1 7.8 %reshape.221 = bf16[2,1024,1024]{2,1,0:T(8,128)(2,1)} reshape(bf16[2,8,128,2,512]{4,3,2,1,0:T(2,128)(2,1)} %copy.61) | data formatting | bytes 8388608 | tf_op jit(solution)/shard_map/reshape | solution.py:135
  (92 shorter events, 11.7 us)
Async XLA Ops:
  7.2 15.0 %copy-start = (f32[262144]{0:T(1024)S(1)}, f32[262144]{0:T(1024)}, u32[]{:S(2)}) copy-start(f32[262144]{0:T(1024)} %param.9) | copy-start | bytes 3145732
  7.2 183.9 %all-reduce.16.cloned.1.call-start = ((), (), s32[]{:S(2)}) async-start(), calls=%async_computation.4 | async-start | bytes 4194304
  9.4 2.2 copy-start.20
  10.7 2.4 copy-start.7
  13.2 1.5 copy-start.6
  13.4 2.2 copy-start.13
  14.7 0.8 copy-start.11
  16.1 1.5 copy-start.9
  17.6 1.5 copy-start.15
  17.6 1.5 copy-start.19
  17.8 2.8 copy-start.2
  20.7 1.5 copy-start.22
  25.9 2.5 copy-start.3
  28.4 1.8 copy-start.17
  32.3 2.7 copy-start.21
  32.7 8.5 %copy-start.4 = (bf16[5,128,1024]{2,1,0:T(8,128)(2,1)}, bf16[5,128,1024]{2,1,0:T(8,128)(2,1)S(1)}, u32[]{:S(2)}) copy-start(bf16[5,128,1024]{2,1,0:T(8,128)(2,1)S(1)} %fusion.102) | copy-start | bytes 3932164
  36.7 1.0 copy-start.12
  37.8 1.7 copy-start.14
  40.1 1.1 copy-start.5
  41.6 1.5 copy-start.10
  46.7 1.3 copy-start.8
  52.4 2.4 copy-start.18
  58.1 319.9 %reduce-scatter.2.cloned.1.call-start = ((), (), s32[]{:S(2)}) async-start(), calls=%async_computation.1 | async-start | bytes 8650752 | tf_op jit(solution)/shard_map/reduce_scatter | solution.py:125
  66.9 3.7 copy-start.16
  78.3 360.7 %all-gather.6.cloned.1.call-start = ((), (), s32[]{:S(2)}) async-start(), calls=%async_computation.3 | async-start | bytes 2162688 | tf_op jit(solution)/shard_map/all_gather | solution.py:118
  263.1 241.5 %all-gather.4.cloned.1.call-start = ((), (), s32[]{:S(2)}) async-start(), calls=%async_computation.2 | async-start | bytes 4325376 | tf_op jit(solution)/shard_map/all_gather | solution.py:131
  513.1 7.8 %copy-start.1 = (f32[262144]{0:T(1024)S(1)}, f32[262144]{0:T(1024)}, u32[]{:S(2)}) copy-start(f32[262144]{0:T(1024)} %param.9) | copy-start | bytes 3145732
Sparse Core Ops, SparseCore 0:
  58.2 132.8 all-reduce.15
  193.5 184.4 reduce-scatter.1
  381.9 57.0 all-gather.5
  442.8 61.7 all-gather.3
where the time goes:
time: 535 us; the launch traced here: 528 us
  waiting for transfers between devices  349 us (65%)
  local copies, waits for them, and re-layouts  53 us (10%)
  blocking collectives  44.2 us (8%)
  other arithmetic  36.2 us (7%)
  matrix products  29.1 us (5%)
  between operations  15.4 us (3%)
    reduce_scatter x1, waiting for transfers between devices, shards(): lax.psum_scatter(grad_terms, ('dp', 'layer'), scatter_dimension=0, tiled=...  114 us
    unnamed x5, waiting for transfers between devices  113 us
    all_gather x1, waiting for transfers between devices, shards(): gathered = lax.all_gather(update_block, ('dp', 'layer'), axis=0, tiled=True)  62.1 us
    all_gather x1, waiting for transfers between devices, shards(): lax.all_gather(inverse.reshape(1, block * block), ('dp', 'layer'), axis=0...  59.9 us
    psum x1, blocking collectives, shards(): totals = lax.psum(marked, ('dp', 'layer'))  44.2 us
    unnamed x51, local copies, waits for them, and re-layouts  13.7 us
    another operation x3, other arithmetic, damped_inverse(): lower = jnp.linalg.cholesky(damped)  12.4 us
  transfers between devices with their start and end apart: 4, of which 4 were waited for; matrix products, arithmetic and copies ran while one was open for 9% of the time, Pallas kernels for 0%

commit v1 on v0

--- a/solution.py
+++ b/solution.py
@@ -1,6 +1,10 @@
+import functools
+
 import jax
 import jax.numpy as jnp
 from jax import lax
+from jax.experimental import pallas as pl
+from jax.experimental.pallas import tpu as pltpu
 from jax.sharding import PartitionSpec as P
 
 VISCOSITY = 0.1
@@ -71,6 +75,396 @@
     damped = factor + DAMPING * scale * eye
     lower = jnp.linalg.cholesky(damped)
     return jax.scipy.linalg.cho_solve((lower, True), jnp.broadcast_to(eye, damped.shape))
+
+
+MESH = pl.DeviceIdType.MESH
+TN = (((0,), (0,)), ((), ()))
+
+
+def mm(a, b, dims):
+    return lax.dot_general(a, b, dims, preferred_element_type=jnp.float32)
+
+
+def high(a, b):
+    return jnp.dot(a, b, precision=lax.Precision.HIGHEST, preferred_element_type=jnp.float32)
+
+
+def invert(damped):
+    size = damped.shape[0]
+    row_id = lax.broadcasted_iota(jnp.int32, (size, size), 0)
+    col_id = lax.broadcasted_iota(jnp.int32, (size, size), 1)
+
+    def step(k, a):
+        in_row = row_id == k
+        in_col = col_id == k
+        row = jnp.sum(jnp.where(in_row, a, 0.0), axis=0, keepdims=True)
+        col = jnp.sum(jnp.where(in_col, a, 0.0), axis=1, keepdims=True)
+        pivot = jnp.sum(jnp.where(in_col[:1], row, 0.0), axis=1, keepdims=True)
+        row = jnp.where(in_col[:1], 1.0, row) * (1.0 / pivot)
+        col = jnp.where(in_row[:, :1], -1.0, col)
+        return jnp.where(in_row | in_col, 0.0, a) - col * row
+
+    return lax.fori_loop(0, size, step, damped)
+
+
+def exchange_kernel(
+    n_dp, n_layer, total, *refs
+):
+    levels = n_layer // 2
+    n_chip = n_dp // 2
+    stacks, deltas = refs[:levels], refs[levels : 2 * levels]
+    (out, f_send, f_own, fc_recv, fp_recv, fz_send, fz_recv, tr_send, tr_recv, inv_own, inv_a, inv_g,
+     g_send, g_own, gc_recv, gp_recv, gz_send, gz_recv,
+     s_fc, r_fc, s_fp, r_fp, s_fz, r_fz, s_tr, r_tr, s_ia, r_ia, s_ig, r_ig,
+     s_gc, r_gc, s_gp, r_gp, s_gz, r_gz, s_uz, s_up, s_uc, r_u) = refs[2 * levels :]
+    width = stacks[0].shape[1]
+    block = width // n_dp
+    half = width // 2
+    n_half = n_dp // 2
+    d = lax.axis_index("dp")
+    l = lax.axis_index("layer")
+    chip, core = d // 2, d % 2
+    level, kind = l // 2, l % 2
+    sib = (chip * 2 + 1 - core, l)
+
+    def remote(src, dst, send, recv, dev):
+        return pltpu.make_async_remote_copy(
+            src_ref=src, dst_ref=dst, send_sem=send, recv_sem=recv, device_id=dev, device_id_type=MESH
+        )
+
+    def other(k):
+        return lax.rem(chip + 1 + k, n_chip)
+
+    def loop(n, body):
+        def run(i, carry):
+            body(i)
+            return carry
+
+        lax.fori_loop(0, n, run, 0)
+
+    barrier = pltpu.get_barrier_semaphore()
+
+    def greet(k):
+        to = lax.rem(d + 1 + k, n_dp)
+        pl.semaphore_signal(barrier, inc=1, device_id=(to, l), device_id_type=MESH)
+
+    def greet_mate(k):
+        pl.semaphore_signal(barrier, inc=1, device_id=(k, 2 * level + 1 - kind), device_id_type=MESH)
+
+    def greet_layer(k):
+        to = lax.rem(2 * level + 2 + k, n_layer)
+        pl.semaphore_signal(barrier, inc=1, device_id=(d, to), device_id_type=MESH)
+
+    loop(n_dp - 1, greet)
+    loop(n_dp, greet_mate)
+    loop(n_layer - 2, greet_layer)
+
+    def columns(ref, dp):
+        return ref[:, pl.ds(pl.multiple_of(dp * block, block), block)]
+
+    def factor(lay, dp):
+        rows = columns(stacks[lay // 2] if lay % 2 == 0 else deltas[lay // 2], dp)
+        term = mm(rows, rows, TN)
+        return term / total if lay % 2 == 0 else term * total
+
+    def grad(lay, dp):
+        cols = slice((lay % 2) * half, (lay % 2 + 1) * half)
+        return mm(columns(stacks[lay // 2], dp), deltas[lay // 2][:, cols], TN)
+
+    def fc_copy(c):
+        return remote(f_send.at[c], fc_recv.at[c], s_fc.at[c], r_fc.at[c], sib)
+
+    def gc_copy(c):
+        return remote(g_send.at[c], gc_recv.at[c], s_gc.at[c], r_gc.at[c], sib)
+
+    def fp_copy(c, slot):
+        return remote(f_own.at[c], fp_recv.at[slot], s_fp.at[c], r_fp.at[slot], (2 * c + core, l))
+
+    def gp_copy(c, lay, slot):
+        return remote(
+            g_own.at[c, lay], gp_recv.at[slot, lay], s_gp.at[c, lay], r_gp.at[slot, lay], (2 * c + core, l)
+        )
+
+    def fz_copy(lay, slot):
+        return remote(fz_send.at[lay], fz_recv.at[slot], s_fz.at[lay], r_fz.at[slot], (d, lay))
+
+    def gz_copy(lay, slot):
+        return remote(gz_send.at[lay], gz_recv.at[slot], s_gz.at[lay], r_gz.at[slot], (d, lay))
+
+    def first_factor(k):
+        c = other(k)
+        for lay in range(n_layer):
+            f_send[c, lay] = factor(lay, 2 * c + 1 - core)
+
+    loop(n_chip, first_factor)
+    pl.semaphore_wait(barrier, 2 * n_dp - 1 + n_layer - 2)
+    loop(n_chip, lambda k: fc_copy(other(k)).start())
+
+    def first_grad(k):
+        c = other(k)
+        for lay in range(n_layer):
+            g_send[c, lay] = grad(lay, 2 * c + 1 - core)
+        gc_copy(c).start()
+
+    loop(n_chip, first_grad)
+
+    def second_factor(k):
+        c = other(k)
+        fc_copy(c).wait_recv()
+        for lay in range(n_layer):
+            f_own[c, lay] = factor(lay, 2 * c + core) + fc_recv[c, lay]
+
+    def send_factor(k):
+        second_factor(k)
+        fp_copy(other(k), chip).start()
+
+    loop(n_chip - 1, send_factor)
+    second_factor(n_chip - 1)
+
+    def second_grad(k):
+        c = other(k)
+        gc_copy(c).wait_recv()
+        for lay in range(n_layer):
+            g_own[c, lay] = grad(lay, 2 * c + core) + gc_recv[c, lay]
+
+    def send_grad(k):
+        second_grad(k)
+        loop(n_layer, lambda lay: gp_copy(other(k), lay, chip).start())
+
+    loop(n_chip - 1, send_grad)
+    second_grad(n_chip - 1)
+
+    loop(n_chip - 1, lambda k: fp_copy(other(k), other(k)).wait_recv())
+
+    def plane_factor(lay):
+        value = f_own[chip, lay]
+        for k in range(n_chip - 1):
+            value = value + fp_recv[other(k), lay]
+        fz_send[lay] = value
+
+    def send_plane_factor(k):
+        lay = lax.rem(l + 1 + k, n_layer)
+        plane_factor(lay)
+        fz_copy(lay, l).start()
+
+    loop(n_layer - 1, send_plane_factor)
+    plane_factor(l)
+    mine = fz_send[l]
+    for k in range(n_layer - 1):
+        lay = lax.rem(l + 1 + k, n_layer)
+        fz_copy(lay, lay).wait_recv()
+        mine = mine + fz_recv[lay]
+
+    diagonal = lax.broadcasted_iota(jnp.int32, (block, block), 0) == lax.broadcasted_iota(
+        jnp.int32, (block, block), 1
+    )
+    trace = jnp.sum(jnp.sum(jnp.where(diagonal, mine, 0.0), axis=0, keepdims=True), axis=1, keepdims=True)
+    tr_send[...] = jnp.broadcast_to(trace, tr_send.shape)
+
+    def tr_copy(to, slot):
+        return remote(tr_send, tr_recv.at[slot], s_tr.at[to], r_tr.at[slot], (to, l))
+
+    loop(n_dp - 1, lambda k: tr_copy(lax.rem(d + 1 + k, n_dp), d).start())
+    traces = tr_send[...]
+    for k in range(n_dp - 1):
+        to = lax.rem(d + 1 + k, n_dp)
+        tr_copy(to, to).wait_recv()
+        traces = traces + tr_recv[to]
+    damped = mine + jnp.where(diagonal, DAMPING / width * traces[:1], 0.0)
+    inv_own[...] = invert(damped)
+
+    def ia_copy():
+        return remote(inv_own, inv_a, s_ia, r_ia, (d, 2 * level + 1))
+
+    def ig_copy(to, lay, slot):
+        return remote(inv_own, inv_g.at[slot], s_ig.at[to], r_ig.at[slot], (to, lay))
+
+    user = 2 * level + d // n_half
+
+    @pl.when(kind == 0)
+    def _():
+        ia_copy().start()
+        inv_a[...] = inv_own[...]
+
+    @pl.when(kind == 1)
+    def _():
+        loop(n_dp - 1, lambda k: ig_copy(lax.rem(d + 1 + k, n_dp), user, d % n_half).start())
+
+        @pl.when(user == l)
+        def _():
+            inv_g[d % n_half] = inv_own[...]
+
+        @pl.when(user != l)
+        def _():
+            ig_copy(d, user, d % n_half).start()
+
+    def plane_grad(lay):
+        value = g_own[chip, lay]
+        for k in range(n_chip - 1):
+            gp_copy(other(k), lay, other(k)).wait_recv()
+            value = value + gp_recv[other(k), lay]
+        gz_send[lay] = value
+
+    def send_plane_grad(lay):
+        plane_grad(lay)
+
+        @pl.when(lay != l)
+        def _():
+            gz_copy(lay, l).start()
+
+    loop(n_layer, send_plane_grad)
+    own = gz_send[l]
+    for k in range(n_layer - 1):
+        lay = lax.rem(l + 1 + k, n_layer)
+        gz_copy(lay, lay).wait_recv()
+        own = own + gz_recv[lay]
+
+    @pl.when(kind == 1)
+    def _():
+        ia_copy().wait_recv()
+
+    def wait_inverse(slot):
+        @pl.when(jnp.logical_or(kind == 0, kind * n_half + slot != d))
+        def _():
+            ig_copy(d, l, slot).wait_recv()
+
+    loop(n_half, wait_inverse)
+
+    def piece(dp, lay):
+        return out.at[
+            lay // 2,
+            pl.ds(pl.multiple_of(dp * block, block), block),
+            pl.ds(pl.multiple_of((lay % 2) * half, half), half),
+        ]
+
+    left = high(inv_a[...], own)
+    for j in range(n_half):
+        value = high(left[:, j * block : (j + 1) * block], inv_g[j]).astype(jnp.bfloat16)
+        out[
+            level,
+            pl.ds(pl.multiple_of(d * block, block), block),
+            pl.ds(pl.multiple_of(kind * half + j * block, block), block),
+        ] = value
+
+    def uz_copy(lay, of):
+        return remote(piece(d, of), piece(d, of), s_uz.at[lay], r_u.at[d, of], (d, lay))
+
+    def up_copy(c, lay, of):
+        return remote(piece(of, lay), piece(of, lay), s_up.at[c, lay], r_u.at[of, lay], (2 * c + core, l))
+
+    def uc_copy(of, lay):
+        return remote(piece(of, lay), piece(of, lay), s_uc.at[of // 2, lay], r_u.at[of, lay], sib)
+
+    def forward(lay):
+        loop(n_chip - 1, lambda k: up_copy(other(k), lay, d).start())
+        uc_copy(d, lay).start()
+
+    loop(n_layer - 1, lambda k: uz_copy(lax.rem(l + 1 + k, n_layer), l).start())
+    forward(l)
+
+    def pass_on(k):
+        lay = lax.rem(l + 1 + k, n_layer)
+        uz_copy(lay, lay).wait_recv()
+        forward(lay)
+
+    loop(n_layer - 1, pass_on)
+
+    def to_sibling(i):
+        of = 2 * other(i // n_layer) + core
+        lay = lax.rem(l + i % n_layer, n_layer)
+        up_copy(other(i // n_layer), lay, of).wait_recv()
+        uc_copy(of, lay).start()
+
+    loop((n_chip - 1) * n_layer, to_sibling)
+    loop(n_chip * n_layer, lambda i: uc_copy(2 * (i // n_layer) + 1 - core, i % n_layer).wait_recv())
+
+    def sent_chip(c):
+        fc_copy(c).wait_send()
+        gc_copy(c).wait_send()
+        loop(n_layer, lambda lay: uc_copy(2 * c + core, lay).wait_send())
+
+    def sent_plane(k):
+        c = other(k)
+        fp_copy(c, chip).wait_send()
+
+        def sent(lay):
+            gp_copy(c, lay, chip).wait_send()
+            up_copy(c, lay, d).wait_send()
+
+        loop(n_layer, sent)
+
+    def sent_layer(k):
+        lay = lax.rem(l + 1 + k, n_layer)
+        fz_copy(lay, l).wait_send()
+        gz_copy(lay, l).wait_send()
+        uz_copy(lay, l).wait_send()
+
+    loop(n_chip, sent_chip)
+    loop(n_chip - 1, sent_plane)
+    loop(n_layer - 1, sent_layer)
+    loop(n_dp - 1, lambda k: tr_copy(lax.rem(d + 1 + k, n_dp), d).wait_send())
+
+    @pl.when(kind == 0)
+    def _():
+        ia_copy().wait_send()
+
+    @pl.when(kind == 1)
+    def _():
+        loop(n_dp - 1, lambda k: ig_copy(lax.rem(d + 1 + k, n_dp), user, d % n_half).wait_send())
+
+        @pl.when(user != l)
+        def _():
+            ig_copy(d, user, d % n_half).wait_send()
+
+
+def exchange(stacks, deltas, n_dp, n_layer, total):
+    levels = len(stacks)
+    width = stacks[0].shape[1]
+    block, half = width // n_dp, width // 2
+    n_chip = n_dp // 2
+    f32, bf16 = jnp.float32, jnp.bfloat16
+    dma = pltpu.SemaphoreType.DMA
+    factors, grads = (n_layer, block, block), (n_layer, block, half)
+    scratch = [
+        pltpu.VMEM((n_chip, *factors), f32),
+        pltpu.VMEM((n_chip, *factors), f32),
+        pltpu.VMEM((n_chip, *factors), f32),
+        pltpu.VMEM((n_chip, *factors), f32),
+        pltpu.VMEM(factors, f32),
+        pltpu.VMEM(factors, f32),
+        pltpu.VMEM((8, 128), f32),
+        pltpu.VMEM((n_dp, 8, 128), f32),
+        pltpu.VMEM((block, block), f32),
+        pltpu.VMEM((block, block), f32),
+        pltpu.VMEM((n_dp // 2, block, block), f32),
+        pltpu.VMEM((n_chip, *grads), f32),
+        pltpu.VMEM((n_chip, *grads), f32),
+        pltpu.VMEM((n_chip, *grads), f32),
+        pltpu.VMEM((n_chip, *grads), f32),
+        pltpu.VMEM(grads, f32),
+        pltpu.VMEM(grads, f32),
+        dma((n_chip,)), dma((n_chip,)),
+        dma((n_chip,)), dma((n_chip,)),
+        dma((n_layer,)), dma((n_layer,)),
+        dma((n_dp,)), dma((n_dp,)),
+        dma, dma,
+        dma((n_dp,)), dma((n_dp // 2,)),
+        dma((n_chip,)), dma((n_chip,)),
+        dma((n_chip, n_layer)), dma((n_chip, n_layer)),
+        dma((n_layer,)), dma((n_layer,)),
+        dma((n_layer,)), dma((n_chip, n_layer)), dma((n_chip, n_layer)), dma((n_dp, n_layer)),
+    ]
+    return pl.pallas_call(
+        functools.partial(exchange_kernel, n_dp, n_layer, float(total)),
+        out_shape=jax.ShapeDtypeStruct((levels, width, width), bf16),
+        in_specs=[pl.BlockSpec(memory_space=pltpu.VMEM)] * (2 * levels),
+        out_specs=pl.BlockSpec(memory_space=pltpu.VMEM),
+        scratch_shapes=scratch,
+        compiler_params=pltpu.CompilerParams(
+            collective_id=0, has_side_effects=True, vmem_limit_bytes=48 * 2**20
+        ),
+        name="exchange",
+    )(*stacks, *deltas)
 
 
 def shards(coords, sample_ids, pool, in_weight, in_bias, hidden, out_weight):
@@ -90,6 +484,8 @@
     losses, stacks, deltas = point_terms(
         coords, weight, in_weight, in_bias, hidden, out_weight, total
     )
+    if block % 128 == 0 and n_layer == 2 * levels:
+        return (exchange(stacks, deltas, n_dp, n_layer, total), losses)
     factor_list = []
     grad_list = []
     for level in range(levels):

time: 535 us -> 175 us (0.33); the launches traced: 528 us -> 175 us
  waiting for transfers between devices: 349 us -> 0 us
  Pallas kernels: 0 us -> 148 us
  local copies, waits for them, and re-layouts: 53 us -> 8.54 us
  blocking collectives: 44.2 us -> 0 us
  other arithmetic: 36.2 us -> 5.68 us
  matrix products: 29.1 us -> 11.9 us
  between operations: 15.4 us -> 0.91 us
    pallas_call x0 -> x1, Pallas kernels: none -> 148 us  [exchange(): pl.pallas_call(functools.partial(exchange_kernel, n_dp, n_layer, float(to...]
    all_gather x2 -> x0, waiting for transfers between devices: 122 us -> none  [the longest x1 62.1 us: shards(): gathered = lax.all_gather(update_block, ('dp', 'layer'), axis=0, tiled=True)]
    reduce_scatter x1 -> x0, waiting for transfers between devices: 114 us -> none  [shards(): lax.psum_scatter(grad_terms, ('dp', 'layer'), scatter_dimension=0, tiled=...]
    unnamed x5 -> x0, waiting for transfers between devices: 113 us -> none
    psum x1 -> x0, blocking collectives: 44.2 us -> none  [shards(): totals = lax.psum(marked, ('dp', 'layer'))]
    another operation x8 -> x0, other arithmetic: 24.8 us -> none  [the longest x3 12.4 us: damped_inverse(): lower = jnp.linalg.cholesky(damped)]
    convert_element_type x5 -> x0, local copies, waits for them, and re-layouts: 14.7 us -> none  [the longest x2 8.77 us: point_terms(): piece.astype(jnp.bfloat16)]
    dot_general x8 -> x0, matrix products: 13.5 us -> none  [the longest x2 5.48 us: shards(): jnp.einsum('rnb,rhc->nhbc', rows_a, halves, preferred_element_type=jnp.fl...]
  transfers between devices with their start and end apart: 4 -> 0, of which waited for: 4 -> 0; matrix products, arithmetic and copies ran while one was open for 9% -> 0% of each run, Pallas kernels for 0% -> 0%
where the time goes in v1:
time: 175 us
  Pallas kernels  148 us (85%)
  matrix products  11.9 us (7%)
  local copies, waits for them, and re-layouts  8.54 us (5%)
  other arithmetic  5.68 us (3%)
    pallas_call x1, Pallas kernels, exchange(): pl.pallas_call(functools.partial(exchange_kernel, n_dp, n_layer, float(to...  148 us
    unnamed x9, local copies, waits for them, and re-layouts  7.01 us
    dot_general x3, matrix products, network(): jnp.dot(stack, hidden[level], preferred_element_type=jnp.float32)  4.64 us

profile of v1, /device:TPU:9, one launch (start us, length us, event | category | flops | bytes accessed | tf_op | source)
XLA Modules:
  0.0 174.8 jit_solution(9108906024943687900)
XLA Ops:
  0.6 0.0 copy-start
  0.6 0.0 copy-start.2
  0.7 0.7 compare_select_fusion.2
  1.4 0.5 copy-done
  1.9 1.1 gather_fusion
  3.0 0.7 multiply_reduce_fusion.4
  3.8 1.4 multiply_subtract_fusion.2
  5.2 0.1 subtract_bitcast_fusion.1
  5.3 0.0 copy-done.2
  5.3 0.0 copy-start.3
  5.3 0.1 broadcast_multiply_fusion.1
  5.5 0.2 maximum_convert_fusion
  5.6 1.9 %copy-done.3 = bf16[2,1024,1024]{2,1,0:T(8,128)(2,1)S(1)} copy-done((bf16[2,1024,1024]{2,1,0:T(8,128)(2,1)S(1)}, bf16[2,1024,1024]{2,1,0:T(8,128)(2,1)}, u32[]{:S(2)}) %copy-start.3) | copy-done | bytes 4194328
  7.5 1.5 fusion.4
  9.0 0.1 multiply_subtract_fusion.1
  9.1 0.2 slice.80
  9.3 0.2 multiply_reduce_fusion.3
  9.5 0.2 fusion.32
  9.7 0.2 broadcast_multiply_fusion
  9.9 0.2 maximum_convert_fusion.1
  10.1 0.0 copy-start.1
  10.1 1.5 fusion.2
  11.6 0.0 copy-done.1
  11.6 0.5 convolution_bitcast_fusion
  12.2 0.1 multiply_subtract_fusion
  12.3 0.1 slice.83
  12.4 1.4 fusion.15
  13.9 0.2 multiply_reduce_fusion.2
  14.0 0.7 negate_multiply_fusion.2
  14.7 0.5 fusion.54
  15.3 0.6 fusion.49
  15.9 0.2 multiply_bitcast_fusion.1
  16.1 1.8 %add_add_fusion.1 = (f32[3,128,1024]{2,1,0:T(8,128)S(1)}, f32[128,1024]{1,0:T(8,128)S(1)}) fusion(f32[3,128,1024]{2,1,0:T(8,128)S(1)} %bitcast.95, f32[128,1024]{1,0:T(8,128)S(1)} %get-tuple-element.10, f32[128,1024]{1,0:T(8,128)S(1)} %multiply_subtract_fusion, f32[1024,4]{0,1:T(4,128)S(1)} %copy-done.1, f32[3,128,3]{1,2,0:T(4,128)S(1)} %get-tuple-element.16, ...), kind=kOutput, calls=%fused_computation.6 | convolution fusion | flops 21108736 | bytes 4741632 | tf_op jit(solution)/shard_map/transpose(jvp(kpw,wc->kpc))/dot_general | solution.py:41
  17.9 0.9 fusion.20
  18.8 0.2 pad_add_fusion
  19.0 1.6 fusion.12
  20.6 0.1 split.16
  20.7 0.4 multiply_reduce_fusion
  21.0 0.4 multiply_bitcast_fusion
  21.5 0.7 add_add_fusion
  22.2 0.2 add_convert_fusion
  22.4 147.8 %exchange.1 = bf16[2,1024,1024]{2,1,0:T(8,128)(2,1)} custom-call(bf16[640,1024]{1,0:T(8,128)(2,1)S(1)} %bitcast.83, bf16[640,1024]{1,0:T(8,128)(2,1)S(1)} %bitcast.85, bf16[640,1024]{1,0:T(8,128)(2,1)S(1)} %bitcast.88, bf16[640,1024]{1,0:T(8,128)(2,1)S(1)} %bitcast.87), custom_call_target="tpu_custom_call" | custom-call | tf_op jit(solution)/shard_map/exchange/pallas_call | solution.py:457
  170.2 4.6 %copy.18 = bf16[2,1024,1024]{2,1,0:T(8,128)(2,1)} copy(bf16[2,1024,1024]{2,1,0:T(8,128)(2,1)} %exchange.1) | data formatting | bytes 8388608
  (7 shorter events, 0.1 us)
Async XLA Ops:
  0.6 1.2 copy-start
  0.6 4.7 %copy-start.2 = (f32[3,1024]{1,0:T(4,128)S(1)}, f32[3,1024]{1,0:T(4,128)}, u32[]{:S(2)}) copy-start(f32[3,1024]{1,0:T(4,128)} %param.10) | copy-start | bytes 36868
  5.3 2.2 %copy-start.3 = (bf16[2,1024,1024]{2,1,0:T(8,128)(2,1)S(1)}, bf16[2,1024,1024]{2,1,0:T(8,128)(2,1)}, u32[]{:S(2)}) copy-start(bf16[2,1024,1024]{2,1,0:T(8,128)(2,1)} %param.12) | copy-start | bytes 12582916
  10.1 1.6 copy-start.1

commit v2 on v1

--- a/solution.py
+++ b/solution.py
@@ -89,7 +89,7 @@
     return jnp.dot(a, b, precision=lax.Precision.HIGHEST, preferred_element_type=jnp.float32)
 
 
-def invert(damped):
+def eliminate(damped, first, last):
     size = damped.shape[0]
     row_id = lax.broadcasted_iota(jnp.int32, (size, size), 0)
     col_id = lax.broadcasted_iota(jnp.int32, (size, size), 1)
@@ -104,7 +104,7 @@
         col = jnp.where(in_row[:, :1], -1.0, col)
         return jnp.where(in_row | in_col, 0.0, a) - col * row
 
-    return lax.fori_loop(0, size, step, damped)
+    return lax.fori_loop(first, last, step, damped)
 
 
 def exchange_kernel(
@@ -116,7 +116,7 @@
     (out, f_send, f_own, fc_recv, fp_recv, fz_send, fz_recv, tr_send, tr_recv, inv_own, inv_a, inv_g,
      g_send, g_own, gc_recv, gp_recv, gz_send, gz_recv,
      s_fc, r_fc, s_fp, r_fp, s_fz, r_fz, s_tr, r_tr, s_ia, r_ia, s_ig, r_ig,
-     s_gc, r_gc, s_gp, r_gp, s_gz, r_gz, s_uz, s_up, s_uc, r_u) = refs[2 * levels :]
+     s_gc, r_gc, s_gp, r_gp, s_gz, r_gz, s_uz, s_up, s_uc, r_u, s_ga, r_ga, s_uf) = refs[2 * levels :]
     width = stacks[0].shape[1]
     block = width // n_dp
     half = width // 2
@@ -126,6 +126,10 @@
     chip, core = d // 2, d % 2
     level, kind = l // 2, l % 2
     sib = (chip * 2 + 1 - core, l)
+    near_x = chip + 1 - 2 * (chip % 2)
+    near_y = lax.rem(chip + 2, n_chip)
+    across = n_chip - 1 - chip
+    quarter = half // 2
 
     def remote(src, dst, send, recv, dev):
         return pltpu.make_async_remote_copy(
@@ -227,12 +231,39 @@
         for lay in range(n_layer):
             g_own[c, lay] = grad(lay, 2 * c + core) + gc_recv[c, lay]
 
-    def send_grad(k):
-        second_grad(k)
-        loop(n_layer, lambda lay: gp_copy(other(k), lay, chip).start())
-
-    loop(n_chip - 1, send_grad)
-    second_grad(n_chip - 1)
+    loop(n_chip, second_grad)
+
+    def turn(k):
+        return lax.rem(l + 1 + k, n_layer)
+
+    def ga_copy(way, lay):
+        to, slot = ((near_x, near_y), (near_y, near_x))[way]
+        cols = pl.ds(way * quarter, quarter)
+        return remote(
+            g_own.at[across, lay, :, cols], gp_recv.at[slot, lay, :, cols],
+            s_ga.at[way, lay], r_ga.at[way, lay], (2 * to + core, l),
+        )
+
+    def start_across(k):
+        ga_copy(0, turn(k)).start()
+        ga_copy(1, turn(k)).start()
+
+    loop(n_layer, start_across)
+
+    def arrived_across(way, lay):
+        cols = pl.ds(way * quarter, quarter)
+        return remote(
+            g_own.at[across, lay, :, cols], gp_recv.at[across, lay, :, cols],
+            s_ga.at[way, lay], r_ga.at[way, lay], (2 * near_x + core, l),
+        )
+
+    def relay(k):
+        lay = turn(k)
+        for way, to in ((0, near_y), (1, near_x)):
+            cols = slice(way * quarter, (way + 1) * quarter)
+            arrived_across(way, lay).wait_recv()
+            g_own[to, lay, :, cols] = g_own[to, lay, :, cols] + gp_recv[across, lay, :, cols]
+            gp_copy(to, lay, chip).start()
 
     loop(n_chip - 1, lambda k: fp_copy(other(k), other(k)).wait_recv())
 
@@ -249,6 +280,7 @@
 
     loop(n_layer - 1, send_plane_factor)
     plane_factor(l)
+    loop(n_layer // 2, relay)
     mine = fz_send[l]
     for k in range(n_layer - 1):
         lay = lax.rem(l + 1 + k, n_layer)
@@ -265,13 +297,31 @@
         return remote(tr_send, tr_recv.at[slot], s_tr.at[to], r_tr.at[slot], (to, l))
 
     loop(n_dp - 1, lambda k: tr_copy(lax.rem(d + 1 + k, n_dp), d).start())
+    loop(n_layer - n_layer // 2, lambda k: relay(n_layer // 2 + k))
     traces = tr_send[...]
     for k in range(n_dp - 1):
         to = lax.rem(d + 1 + k, n_dp)
         tr_copy(to, to).wait_recv()
         traces = traces + tr_recv[to]
     damped = mine + jnp.where(diagonal, DAMPING / width * traces[:1], 0.0)
-    inv_own[...] = invert(damped)
+
+    def plane_grad(lay):
+        value = g_own[chip, lay]
+        for c in (near_x, near_y):
+            gp_copy(c, lay, c).wait_recv()
+            value = value + gp_recv[c, lay]
+        gz_send[lay] = value
+
+    def send_plane_grad(k):
+        plane_grad(turn(k))
+        gz_copy(turn(k), l).start()
+
+    early = n_layer // 2
+    part = block // (early + 1)
+    for k in range(early):
+        damped = eliminate(damped, k * part, (k + 1) * part)
+        send_plane_grad(k)
+    inv_own[...] = eliminate(damped, early * part, block)
 
     def ia_copy():
         return remote(inv_own, inv_a, s_ia, r_ia, (d, 2 * level + 1))
@@ -298,21 +348,9 @@
         def _():
             ig_copy(d, user, d % n_half).start()
 
-    def plane_grad(lay):
-        value = g_own[chip, lay]
-        for k in range(n_chip - 1):
-            gp_copy(other(k), lay, other(k)).wait_recv()
-            value = value + gp_recv[other(k), lay]
-        gz_send[lay] = value
-
-    def send_plane_grad(lay):
-        plane_grad(lay)
-
-        @pl.when(lay != l)
-        def _():
-            gz_copy(lay, l).start()
-
-    loop(n_layer, send_plane_grad)
+    for k in range(early, n_layer - 1):
+        send_plane_grad(k)
+    plane_grad(l)
     own = gz_send[l]
     for k in range(n_layer - 1):
         lay = lax.rem(l + 1 + k, n_layer)
@@ -356,7 +394,8 @@
         return remote(piece(of, lay), piece(of, lay), s_uc.at[of // 2, lay], r_u.at[of, lay], sib)
 
     def forward(lay):
-        loop(n_chip - 1, lambda k: up_copy(other(k), lay, d).start())
+        up_copy(near_x, lay, d).start()
+        up_copy(near_y, lay, d).start()
         uc_copy(d, lay).start()
 
     loop(n_layer - 1, lambda k: uz_copy(lax.rem(l + 1 + k, n_layer), l).start())
@@ -369,13 +408,36 @@
 
     loop(n_layer - 1, pass_on)
 
-    def to_sibling(i):
-        of = 2 * other(i // n_layer) + core
-        lay = lax.rem(l + i % n_layer, n_layer)
-        up_copy(other(i // n_layer), lay, of).wait_recv()
+    def uf_copy(to, of, lay):
+        return remote(piece(of, lay), piece(of, lay), s_uf.at[lay], r_u.at[of, lay], (2 * to + core, l))
+
+    def from_near(k):
+        lay = lax.rem(l + k, n_layer)
+        of_x, of_y = 2 * near_x + core, 2 * near_y + core
+        up_copy(near_x, lay, of_x).wait_recv()
+
+        @pl.when(lay % 2 == 0)
+        def _():
+            uf_copy(near_y, of_x, lay).start()
+
+        uc_copy(of_x, lay).start()
+        up_copy(near_y, lay, of_y).wait_recv()
+
+        @pl.when(lay % 2 == 1)
+        def _():
+            uf_copy(near_x, of_y, lay).start()
+
+        uc_copy(of_y, lay).start()
+
+    loop(n_layer, from_near)
+
+    def from_across(k):
+        lay = lax.rem(l + k, n_layer)
+        of = 2 * across + core
+        uf_copy(near_x, of, lay).wait_recv()
         uc_copy(of, lay).start()
 
-    loop((n_chip - 1) * n_layer, to_sibling)
+    loop(n_layer, from_across)
     loop(n_chip * n_layer, lambda i: uc_copy(2 * (i // n_layer) + 1 - core, i % n_layer).wait_recv())
 
     def sent_chip(c):
@@ -387,11 +449,12 @@
         c = other(k)
         fp_copy(c, chip).wait_send()
 
-        def sent(lay):
+    def sent_near(lay):
+        for way, c in ((0, near_x), (1, near_y)):
+            ga_copy(way, lay).wait_send()
             gp_copy(c, lay, chip).wait_send()
             up_copy(c, lay, d).wait_send()
-
-        loop(n_layer, sent)
+        uf_copy(near_x, d, lay).wait_send()
 
     def sent_layer(k):
         lay = lax.rem(l + 1 + k, n_layer)
@@ -401,6 +464,7 @@
 
     loop(n_chip, sent_chip)
     loop(n_chip - 1, sent_plane)
+    loop(n_layer, sent_near)
     loop(n_layer - 1, sent_layer)
     loop(n_dp - 1, lambda k: tr_copy(lax.rem(d + 1 + k, n_dp), d).wait_send())
 
@@ -453,6 +517,7 @@
         dma((n_chip, n_layer)), dma((n_chip, n_layer)),
         dma((n_layer,)), dma((n_layer,)),
         dma((n_layer,)), dma((n_chip, n_layer)), dma((n_chip, n_layer)), dma((n_dp, n_layer)),
+        dma((2, n_layer)), dma((2, n_layer)), dma((n_layer,)),
     ]
     return pl.pallas_call(
         functools.partial(exchange_kernel, n_dp, n_layer, float(total)),
@@ -484,7 +549,7 @@
     losses, stacks, deltas = point_terms(
         coords, weight, in_weight, in_bias, hidden, out_weight, total
     )
-    if block % 128 == 0 and n_layer == 2 * levels:
+    if block % 128 == 0 and n_dp == 8 and n_layer == 2 * levels:
         return (exchange(stacks, deltas, n_dp, n_layer, total), losses)
     factor_list = []
     grad_list = []

time: 175 us -> 142 us (0.81); the launches traced: 175 us -> 139 us
  Pallas kernels: 148 us -> 112 us
    pallas_call x1, Pallas kernels: 148 us -> 112 us  [exchange(): pl.pallas_call(functools.partial(exchange_kernel, n_dp, n_layer, float(to...]
where the time goes in v2:
time: 142 us; the launch traced here: 139 us
  Pallas kernels  112 us (79%)
  matrix products  11.9 us (8%)
  local copies, waits for them, and re-layouts  8.54 us (6%)
  other arithmetic  5.68 us (4%)
    pallas_call x1, Pallas kernels, exchange(): pl.pallas_call(functools.partial(exchange_kernel, n_dp, n_layer, float(to...  112 us
    unnamed x9, local copies, waits for them, and re-layouts  7.01 us
    dot_general x3, matrix products, network(): jnp.dot(stack, hidden[level], preferred_element_type=jnp.float32)  4.64 us
    dot_general x2, matrix products, network(): jnp.einsum('kpw,wc->kpc', act_grad, out_weight, precision=lax.Precision.H...  3.2 us

profile of v2, /device:TPU:9, one launch (start us, length us, event | category | flops | bytes accessed | tf_op | source)
XLA Modules:
  0.0 139.1 jit_solution(16494005397342787134)
XLA Ops:
  0.6 0.0 copy-start
  0.6 0.0 copy-start.2
  0.7 0.7 compare_select_fusion.2
  1.4 0.5 copy-done
  1.9 1.1 gather_fusion
  3.0 0.7 multiply_reduce_fusion.4
  3.8 1.4 multiply_subtract_fusion.2
  5.2 0.1 subtract_bitcast_fusion.1
  5.3 0.0 copy-done.2
  5.3 0.0 copy-start.3
  5.3 0.1 broadcast_multiply_fusion.1
  5.5 0.2 maximum_convert_fusion
  5.6 1.9 %copy-done.3 = bf16[2,1024,1024]{2,1,0:T(8,128)(2,1)S(1)} copy-done((bf16[2,1024,1024]{2,1,0:T(8,128)(2,1)S(1)}, bf16[2,1024,1024]{2,1,0:T(8,128)(2,1)}, u32[]{:S(2)}) %copy-start.3) | copy-done | bytes 4194328
  7.5 1.5 %fusion.4 = f32[640,1024]{1,0:T(8,128)S(1)} fusion(bf16[640,1024]{1,0:T(8,128)(2,1)S(1)} %bitcast.82, bf16[2,1024,1024]{2,1,0:T(8,128)(2,1)S(1)} %copy-done.3), kind=kOutput, calls=%fused_computation.11 | convolution fusion | flops 1342177280 | bytes 6029312 | tf_op jit(solution)/shard_map/jvp()/dot_general | solution.py:36
  9.0 0.1 multiply_subtract_fusion.1
  9.1 0.2 slice.80
  9.3 0.2 multiply_reduce_fusion.3
  9.5 0.2 fusion.32
  9.7 0.2 broadcast_multiply_fusion
  9.9 0.2 maximum_convert_fusion.1
  10.1 0.0 copy-start.1
  10.1 1.5 %fusion.2 = f32[640,1024]{1,0:T(8,128)S(1)} fusion(bf16[640,1024]{1,0:T(8,128)(2,1)S(1)} %bitcast.84, bf16[2,1024,1024]{2,1,0:T(8,128)(2,1)S(1)} %copy-done.3), kind=kOutput, calls=%fused_computation.9 | convolution fusion | flops 1342177280 | bytes 6029312 | tf_op jit(solution)/shard_map/jvp()/dot_general | solution.py:36
  11.6 0.0 copy-done.1
  11.6 0.5 convolution_bitcast_fusion
  12.2 0.1 multiply_subtract_fusion
  12.3 0.1 slice.83
  12.4 1.4 %fusion.15 = f32[3,128,4]{1,2,0:T(4,128)S(1)} fusion(f32[3,128,1024]{2,1,0:T(8,128)S(1)} %bitcast.93, f32[128,1024]{1,0:T(8,128)S(1)} %multiply_subtract_fusion, f32[1024,4]{0,1:T(4,128)S(1)} %copy-done.1), kind=kOutput, calls=%fused_computation.21 | convolution fusion | flops 19267584 | bytes 2119680 | tf_op jit(solution)/shard_map/jvp(kpw,wc->kpc)/dot_general | solution.py:41
  13.9 0.2 multiply_reduce_fusion.2
  14.0 0.7 negate_multiply_fusion.2
  14.7 0.5 fusion.54
  15.3 0.6 fusion.49
  15.9 0.2 multiply_bitcast_fusion.1
  16.1 1.8 %add_add_fusion.1 = (f32[3,128,1024]{2,1,0:T(8,128)S(1)}, f32[128,1024]{1,0:T(8,128)S(1)}) fusion(f32[3,128,1024]{2,1,0:T(8,128)S(1)} %bitcast.95, f32[128,1024]{1,0:T(8,128)S(1)} %get-tuple-element.10, f32[128,1024]{1,0:T(8,128)S(1)} %multiply_subtract_fusion, f32[1024,4]{0,1:T(4,128)S(1)} %copy-done.1, f32[3,128,3]{1,2,0:T(4,128)S(1)} %get-tuple-element.16, ...), kind=kOutput, calls=%fused_computation.6 | convolution fusion | flops 21108736 | bytes 4741632 | tf_op jit(solution)/shard_map/transpose(jvp(kpw,wc->kpc))/dot_general | solution.py:41
  17.9 0.9 fusion.20
  18.8 0.2 pad_add_fusion
  19.0 1.6 %fusion.12 = f32[640,1024]{1,0:T(8,128)S(1)} fusion(bf16[640,1024]{1,0:T(8,128)(2,1)S(1)} %bitcast.86, bf16[2,1024,1024]{2,1,0:T(8,128)(2,1)S(1)} %copy-done.3), kind=kOutput, calls=%fused_computation.17 | convolution fusion | flops 1342832640 | bytes 6029312 | tf_op jit(solution)/shard_map/transpose(jvp())/dot_general | solution.py:36
  20.6 0.1 split.16
  20.7 0.4 multiply_reduce_fusion
  21.0 0.4 multiply_bitcast_fusion
  21.5 0.7 add_add_fusion
  22.2 0.2 add_convert_fusion
  22.4 112.1 %exchange.1 = bf16[2,1024,1024]{2,1,0:T(8,128)(2,1)} custom-call(bf16[640,1024]{1,0:T(8,128)(2,1)S(1)} %bitcast.83, bf16[640,1024]{1,0:T(8,128)(2,1)S(1)} %bitcast.85, bf16[640,1024]{1,0:T(8,128)(2,1)S(1)} %bitcast.88, bf16[640,1024]{1,0:T(8,128)(2,1)S(1)} %bitcast.87), custom_call_target="tpu_custom_call" | custom-call | tf_op jit(solution)/shard_map/exchange/pallas_call | solution.py:522
  134.5 4.6 %copy.18 = bf16[2,1024,1024]{2,1,0:T(8,128)(2,1)} copy(bf16[2,1024,1024]{2,1,0:T(8,128)(2,1)} %exchange.1) | data formatting | bytes 8388608
  (7 shorter events, 0.1 us)
Async XLA Ops:
  0.6 1.2 copy-start
  0.6 4.7 %copy-start.2 = (f32[3,1024]{1,0:T(4,128)S(1)}, f32[3,1024]{1,0:T(4,128)}, u32[]{:S(2)}) copy-start(f32[3,1024]{1,0:T(4,128)} %param.10) | copy-start | bytes 36868
  5.3 2.2 %copy-start.3 = (bf16[2,1024,1024]{2,1,0:T(8,128)(2,1)S(1)}, bf16[2,1024,1024]{2,1,0:T(8,128)(2,1)}, u32[]{:S(2)}) copy-start(bf16[2,1024,1024]{2,1,0:T(8,128)(2,1)} %param.12) | copy-start | bytes 12582916
  10.1 1.6 %copy-start.1 = (f32[1024,4]{0,1:T(4,128)S(1)}, f32[1024,4]{0,1:T(4,128)}, u32[]{:S(2)}) copy-start(f32[1024,4]{0,1:T(4,128)} %param.13) | copy-start | bytes 49156

commit v3 on v2

--- a/solution.py
+++ b/solution.py
@@ -316,11 +316,11 @@
         plane_grad(turn(k))
         gz_copy(turn(k), l).start()
 
-    early = n_layer // 2
+    early = n_layer - 1
     part = block // (early + 1)
     for k in range(early):
+        send_plane_grad(k)
         damped = eliminate(damped, k * part, (k + 1) * part)
-        send_plane_grad(k)
     inv_own[...] = eliminate(damped, early * part, block)
 
     def ia_copy():

time: 142 us -> 136 us (0.958)
  Pallas kernels: 112 us -> 107 us
    pallas_call x1, Pallas kernels: 112 us -> 107 us  [exchange(): pl.pallas_call(functools.partial(exchange_kernel, n_dp, n_layer, float(to...]
where the time goes in v3:
time: 136 us; the launch traced here: 134 us
  Pallas kernels  107 us (79%)
  matrix products  11.9 us (9%)
  local copies, waits for them, and re-layouts  8.54 us (6%)
  other arithmetic  5.68 us (4%)
    pallas_call x1, Pallas kernels, exchange(): pl.pallas_call(functools.partial(exchange_kernel, n_dp, n_layer, float(to...  107 us
    unnamed x9, local copies, waits for them, and re-layouts  7.01 us
    dot_general x3, matrix products, network(): jnp.dot(stack, hidden[level], preferred_element_type=jnp.float32)  4.64 us
    dot_general x2, matrix products, network(): jnp.einsum('kpw,wc->kpc', act_grad, out_weight, precision=lax.Precision.H...  3.2 us

profile of v3, /device:TPU:9, one launch (start us, length us, event | category | flops | bytes accessed | tf_op | source)
XLA Modules:
  0.0 134.4 jit_solution(10171004931680765918)
XLA Ops:
  0.6 0.0 copy-start
  0.6 0.0 copy-start.2
  0.7 0.7 compare_select_fusion.2
  1.4 0.5 copy-done
  1.9 1.1 gather_fusion
  3.0 0.7 multiply_reduce_fusion.4
  3.8 1.4 %multiply_subtract_fusion.2 = (f32[128,1024]{1,0:T(8,128)S(1)}, f32[128,1024]{1,0:T(8,128)S(1)}) fusion(f32[1024]{0:T(1024)} %param.11, f32[3,128]{1,0:T(4,128)} %param.7, f32[3,1024]{1,0:T(4,128)} %param.10), kind=kOutput, calls=%fused_computation.52 | convolution fusion | flops 5111808 | bytes 1066496 | tf_op jit(solution)/shard_map/jvp()/dot_general | solution.py:24
  5.2 0.1 subtract_bitcast_fusion.1
  5.3 0.0 copy-done.2
  5.3 0.0 copy-start.3
  5.3 0.1 broadcast_multiply_fusion.1
  5.5 0.2 maximum_convert_fusion
  5.6 1.9 %copy-done.3 = bf16[2,1024,1024]{2,1,0:T(8,128)(2,1)S(1)} copy-done((bf16[2,1024,1024]{2,1,0:T(8,128)(2,1)S(1)}, bf16[2,1024,1024]{2,1,0:T(8,128)(2,1)}, u32[]{:S(2)}) %copy-start.3) | copy-done | bytes 4194328
  7.5 1.5 %fusion.4 = f32[640,1024]{1,0:T(8,128)S(1)} fusion(bf16[640,1024]{1,0:T(8,128)(2,1)S(1)} %bitcast.82, bf16[2,1024,1024]{2,1,0:T(8,128)(2,1)S(1)} %copy-done.3), kind=kOutput, calls=%fused_computation.11 | convolution fusion | flops 1342177280 | bytes 6029312 | tf_op jit(solution)/shard_map/jvp()/dot_general | solution.py:36
  9.0 0.1 multiply_subtract_fusion.1
  9.1 0.2 slice.80
  9.3 0.2 multiply_reduce_fusion.3
  9.5 0.2 fusion.32
  9.7 0.2 broadcast_multiply_fusion
  9.9 0.2 maximum_convert_fusion.1
  10.1 0.0 copy-start.1
  10.1 1.5 %fusion.2 = f32[640,1024]{1,0:T(8,128)S(1)} fusion(bf16[640,1024]{1,0:T(8,128)(2,1)S(1)} %bitcast.84, bf16[2,1024,1024]{2,1,0:T(8,128)(2,1)S(1)} %copy-done.3), kind=kOutput, calls=%fused_computation.9 | convolution fusion | flops 1342177280 | bytes 6029312 | tf_op jit(solution)/shard_map/jvp()/dot_general | solution.py:36
  11.6 0.0 copy-done.1
  11.6 0.5 convolution_bitcast_fusion
  12.2 0.1 multiply_subtract_fusion
  12.3 0.1 slice.83
  12.4 1.4 %fusion.15 = f32[3,128,4]{1,2,0:T(4,128)S(1)} fusion(f32[3,128,1024]{2,1,0:T(8,128)S(1)} %bitcast.93, f32[128,1024]{1,0:T(8,128)S(1)} %multiply_subtract_fusion, f32[1024,4]{0,1:T(4,128)S(1)} %copy-done.1), kind=kOutput, calls=%fused_computation.21 | convolution fusion | flops 19267584 | bytes 2119680 | tf_op jit(solution)/shard_map/jvp(kpw,wc->kpc)/dot_general | solution.py:41
  13.9 0.2 multiply_reduce_fusion.2
  14.0 0.7 negate_multiply_fusion.2
  14.7 0.5 fusion.54
  15.3 0.6 fusion.49
  15.9 0.2 multiply_bitcast_fusion.1
  16.1 1.8 %add_add_fusion.1 = (f32[3,128,1024]{2,1,0:T(8,128)S(1)}, f32[128,1024]{1,0:T(8,128)S(1)}) fusion(f32[3,128,1024]{2,1,0:T(8,128)S(1)} %bitcast.95, f32[128,1024]{1,0:T(8,128)S(1)} %get-tuple-element.10, f32[128,1024]{1,0:T(8,128)S(1)} %multiply_subtract_fusion, f32[1024,4]{0,1:T(4,128)S(1)} %copy-done.1, f32[3,128,3]{1,2,0:T(4,128)S(1)} %get-tuple-element.16, ...), kind=kOutput, calls=%fused_computation.6 | convolution fusion | flops 21108736 | bytes 4741632 | tf_op jit(solution)/shard_map/transpose(jvp(kpw,wc->kpc))/dot_general | solution.py:41
  17.9 0.9 fusion.20
  18.8 0.2 pad_add_fusion
  19.0 1.6 %fusion.12 = f32[640,1024]{1,0:T(8,128)S(1)} fusion(bf16[640,1024]{1,0:T(8,128)(2,1)S(1)} %bitcast.86, bf16[2,1024,1024]{2,1,0:T(8,128)(2,1)S(1)} %copy-done.3), kind=kOutput, calls=%fused_computation.17 | convolution fusion | flops 1342832640 | bytes 6029312 | tf_op jit(solution)/shard_map/transpose(jvp())/dot_general | solution.py:36
  20.6 0.1 split.16
  20.7 0.4 multiply_reduce_fusion
  21.0 0.4 multiply_bitcast_fusion
  21.5 0.7 add_add_fusion
  22.2 0.2 add_convert_fusion
  22.4 107.3 %exchange.1 = bf16[2,1024,1024]{2,1,0:T(8,128)(2,1)} custom-call(bf16[640,1024]{1,0:T(8,128)(2,1)S(1)} %bitcast.83, bf16[640,1024]{1,0:T(8,128)(2,1)S(1)} %bitcast.85, bf16[640,1024]{1,0:T(8,128)(2,1)S(1)} %bitcast.88, bf16[640,1024]{1,0:T(8,128)(2,1)S(1)} %bitcast.87), custom_call_target="tpu_custom_call" | custom-call | tf_op jit(solution)/shard_map/exchange/pallas_call | solution.py:522
  129.7 4.6 %copy.18 = bf16[2,1024,1024]{2,1,0:T(8,128)(2,1)} copy(bf16[2,1024,1024]{2,1,0:T(8,128)(2,1)} %exchange.1) | data formatting | bytes 8388608
  (7 shorter events, 0.1 us)
Async XLA Ops:
  0.6 1.2 copy-start
  0.6 4.7 %copy-start.2 = (f32[3,1024]{1,0:T(4,128)S(1)}, f32[3,1024]{1,0:T(4,128)}, u32[]{:S(2)}) copy-start(f32[3,1024]{1,0:T(4,128)} %param.10) | copy-start | bytes 36868
  5.3 2.2 %copy-start.3 = (bf16[2,1024,1024]{2,1,0:T(8,128)(2,1)S(1)}, bf16[2,1024,1024]{2,1,0:T(8,128)(2,1)}, u32[]{:S(2)}) copy-start(bf16[2,1024,1024]{2,1,0:T(8,128)(2,1)} %param.12) | copy-start | bytes 12582916
  10.1 1.6 %copy-start.1 = (f32[1024,4]{0,1:T(4,128)S(1)}, f32[1024,4]{0,1:T(4,128)}, u32[]{:S(2)}) copy-start(f32[1024,4]{0,1:T(4,128)} %param.13) | copy-start | bytes 49156
